TPU v7x, 32 devices: a whole 2x2x4 slice. The times are simulated.
32 devices in a mesh: frow: 4 (over y, x), fcol: 8 (over z, core).
Axes of the slice: x: 2, y: 2, z: 4, core: 2. Of those that a mesh axis runs over, the one named last changes fastest.
Arguments:
- vis: float32 [2, 8192], P(None, ('frow', 'fcol')), may hold values from -6 to 6
- station_pairs: int32 [2, 8192], P(None, ('frow', 'fcol')), may hold values from 0 to 511
- visibility_time_slot: int32 [8192], P(('frow', 'fcol')), may hold values from 0 to 15
- station_u_cells: int32 [512], replicated, may hold values from -1024 to 1023
- station_v_cells: int32 [512], replicated, may hold values from -1024 to 1023
- facet_station_gains: float32 [4, 8, 2, 8192], P('frow', 'fcol'), may hold values from -6 to 6
- holder_device_order: int32 [32], replicated, may hold values from 0 to 31, each once
Outputs:
- image: float32 [4096, 4096], P('frow', 'fcol')
Inputs may be any that keep to these rules, and one draw needn't show every extreme that they name: `holder_device_order`: a permutation; its first 4 entries name distinct devices.
All inputs are finite; a program needn't handle non-finite values.
Results may differ from a plain program's by a relative error of at most 0.0037.
Values sent between devices are 32-bit elements; how exact they have to be, the bound alone decides.
No kernel may reach another device: no remote copies, remote signals or barrier semaphores. Data moves between devices by JAX's collectives and lax.ppermute only.
A program may use at most 64 MiB of HBM per device.

v0:
```python
import math

import jax
import jax.numpy as jnp
from jax import lax
from jax.sharding import PartitionSpec as P

R = 1024
C = 512
M = 64
NT = 16
NBLK = 4


def extended_2(x, sides, width):
    for axis, dim in sides:
        size, length = (lax.axis_size(axis), x.shape[dim])
        up = [(i, (i + 1) % size) for i in range(size - 1)]
        down = [(j, i) for i, j in up]
        last = lax.slice_in_dim(x, length - width, length, axis=dim)
        leading = lax.slice_in_dim(x, 0, width, axis=dim)
        before = lax.ppermute(last, axis, up)
        after = lax.ppermute(leading, axis, down)
        x = jnp.concatenate([before, x, after], axis=dim)
    return x


def taper_line(length):
    index = jnp.arange(length + 2 * M, dtype=jnp.int32).astype(jnp.float32)
    rising = (index + 0.5) / (2.0 * M)
    falling = (length + 2 * M - index - 0.5) / (2.0 * M)
    return jnp.minimum(jnp.minimum(rising, falling), 1.0)


def phase_angles(freq, pixels, modulus):
    cells = jnp.mod(freq, modulus)[None, :] * jnp.mod(pixels, modulus)[:, None] % modulus
    return cells.astype(jnp.float32) * (2.0 * math.pi / modulus)


def block_weights(values, label_names, g_tab, scale):
    first = label_names[0] * NT + label_names[2]
    second = label_names[1] * NT + label_names[2]
    g1r = g_tab[0][first]
    g1i = g_tab[1][first]
    g2r = g_tab[0][second]
    g2i = g_tab[1][second]
    real_gain = g1r * g2r + g1i * g2i
    imag_gain = g1i * g2r - g1r * g2i
    wreal = scale * (values[0] * real_gain - values[1] * imag_gain)
    wimag = scale * (values[0] * imag_gain + values[1] * real_gain)
    return (wreal, wimag)


def fold_columns(field):
    edges = jnp.concatenate([field[:, :M], field[:, -M:]], 1)
    extended = extended_2(edges, (("fcol", 1),), M)
    inner = field[:, M:-M]
    return jnp.concatenate(
        [inner[:, :M] + extended[:, :M], inner[:, M:-M], inner[:, -M:] + extended[:, -M:]], 1
    )


def fold_rows(field):
    edges = jnp.concatenate([field[:M], field[-M:]], 0)
    extended = extended_2(edges, (("frow", 0),), M)
    inner = field[M:-M]
    return jnp.concatenate([inner[:M] + extended[:M], inner[M:-M], inner[-M:] + extended[-M:]], 0)


def shards(
    vis,
    station_pairs,
    visibility_time_slot,
    station_u_cells,
    station_v_cells,
    facet_station_gains,
    holder_device_order,
):
    count_rows = lax.axis_size("frow")
    count_cols = lax.axis_size("fcol")
    n_rows = R * count_rows
    n_cols = C * count_cols
    frow_at = lax.axis_index("frow")
    fcol_at = lax.axis_index("fcol")
    g_tab = facet_station_gains[0, 0]
    label_names = jnp.concatenate([station_pairs, visibility_time_slot[None, :]], 0)
    block_size = vis.shape[1]
    scale = 0.5 / math.sqrt(NBLK * block_size)
    rows = frow_at * R - M + jnp.arange(R + 2 * M, dtype=jnp.int32)
    cols = fcol_at * C - M + jnp.arange(C + 2 * M, dtype=jnp.int32)
    own_flat = frow_at * count_cols + fcol_at
    stacked = jnp.concatenate([vis, label_names.astype(jnp.float32)], 0)
    picked = (holder_device_order[:NBLK] == own_flat)[:, None, None]
    slotted = jnp.where(picked, stacked[None], jnp.zeros((), jnp.float32))
    gathered = lax.psum(slotted, ("frow", "fcol"))
    total = jnp.zeros((R + 2 * M, C + 2 * M), jnp.float32)
    for step in range(NBLK):
        values = gathered[step, :2]
        tag_names = gathered[step, 2:].astype(jnp.int32)
        wreal, wimag = block_weights(values, tag_names, g_tab, scale)
        frequency_u = station_u_cells[tag_names[0]] - station_u_cells[tag_names[1]]
        frequency_v = station_v_cells[tag_names[0]] - station_v_cells[tag_names[1]]
        theta = phase_angles(frequency_u, rows, n_rows)
        phi = phase_angles(frequency_v, cols, n_cols).T
        row_table = jnp.concatenate([jnp.cos(theta), jnp.sin(theta)], 1).astype(jnp.bfloat16)
        top = wreal[:, None] * jnp.cos(phi) - wimag[:, None] * jnp.sin(phi)
        bottom = -(wimag[:, None] * jnp.cos(phi) + wreal[:, None] * jnp.sin(phi))
        col_table = jnp.concatenate([top, bottom], 0).astype(jnp.bfloat16)
        total = total + jnp.dot(row_table, col_table, preferred_element_type=jnp.float32)
    tapered = total * taper_line(R)[:, None] * taper_line(C)[None, :]
    image = fold_rows(fold_columns(tapered))
    return image


def solution(mesh):
    return jax.shard_map(
        shards,
        mesh=mesh,
        in_specs=(
            P(None, ("frow", "fcol")),
            P(None, ("frow", "fcol")),
            P(("frow", "fcol")),
            P(),
            P(),
            P("frow", "fcol", None, None),
            P(),
        ),
        out_specs=P("frow", "fcol"),
        check_vma=False,
    )
```

profile of v0, /device:TPU:12, one launch (start us, length us, event | category | flops | bytes accessed | tf_op | source)
XLA Modules:
  0.0 179.7 jit_solution(15952702674235571813)
XLA Ops:
  2.1 41.3 %psum.7 = f32[4,5,256]{2,1,0:T(8,128)S(1)} all-reduce(f32[4,5,256]{2,1,0:T(8,128)S(1)} %broadcast_select_fusion), channel_id=1, replica_groups=mesh['frow'=4,'fcol'=8] {'frow','fcol'}, use_global_device_ids=true, to_apply=%region_0.1 | all-reduce | flops 5120 | bytes 40960 | tf_op jit(solution)/shard_map/psum | solution.py:95
  72.4 1.9 %gather_fusion.6 = s32[256]{0:T(256)S(1)} fusion(s32[512]{0:T(512)S(1)} %copy-done, s32[1024]{0:T(1024)S(1)} %pad_clamp_fusion.15), kind=kCustom, calls=%fused_computation.6 | custom fusion | bytes 3072 | tf_op jit(solution)/shard_map/gather | solution.py:102
  76.3 1.9 %gather_fusion = s32[256]{0:T(256)S(1)} fusion(s32[512]{0:T(512)S(1)} %copy-done.1, s32[1024]{0:T(1024)S(1)} %pad_clamp_fusion.15), kind=kCustom, calls=%fused_computation | custom fusion | bytes 3072 | tf_op jit(solution)/shard_map/gather | solution.py:101
  78.3 1.9 %gather_fusion.1 = s32[256]{0:T(256)S(1)} fusion(s32[512]{0:T(512)S(1)} %copy-done.1, s32[1024]{0:T(1024)S(1)} %pad_clamp_fusion.14), kind=kCustom, calls=%fused_computation.1 | custom fusion | bytes 3072 | tf_op jit(solution)/shard_map/gather | solution.py:101
  80.2 1.9 %gather_fusion.22 = s32[256]{0:T(256)S(1)} fusion(s32[512]{0:T(512)S(1)} %copy-done, s32[1024]{0:T(1024)S(1)} %pad_clamp_fusion.7), kind=kCustom, calls=%fused_computation.22 | custom fusion | bytes 3072 | tf_op jit(solution)/shard_map/gather | solution.py:102
  82.2 1.9 %gather_fusion.16 = s32[256]{0:T(256)S(1)} fusion(s32[512]{0:T(512)S(1)} %copy-done.1, s32[1024]{0:T(1024)S(1)} %pad_clamp_fusion.7), kind=kCustom, calls=%fused_computation.16 | custom fusion | bytes 3072 | tf_op jit(solution)/shard_map/gather | solution.py:101
  84.1 1.9 %gather_fusion.23 = s32[256]{0:T(256)S(1)} fusion(s32[512]{0:T(512)S(1)} %copy-done, s32[1024]{0:T(1024)S(1)} %pad_clamp_fusion.6), kind=kCustom, calls=%fused_computation.23 | custom fusion | bytes 3072 | tf_op jit(solution)/shard_map/gather | solution.py:102
  86.1 1.9 %gather_fusion.17 = s32[256]{0:T(256)S(1)} fusion(s32[512]{0:T(512)S(1)} %copy-done.1, s32[1024]{0:T(1024)S(1)} %pad_clamp_fusion.6), kind=kCustom, calls=%fused_computation.17 | custom fusion | bytes 3072 | tf_op jit(solution)/shard_map/gather | solution.py:101
  88.1 1.9 %gather_fusion.14 = s32[256]{0:T(256)S(1)} fusion(s32[512]{0:T(512)S(1)} %copy-done, s32[1024]{0:T(1024)S(1)} %pad_clamp_fusion.11), kind=kCustom, calls=%fused_computation.14 | custom fusion | bytes 3072 | tf_op jit(solution)/shard_map/gather | solution.py:102
  90.0 1.9 %gather_fusion.8 = s32[256]{0:T(256)S(1)} fusion(s32[512]{0:T(512)S(1)} %copy-done.1, s32[1024]{0:T(1024)S(1)} %pad_clamp_fusion.11), kind=kCustom, calls=%fused_computation.8 | custom fusion | bytes 3072 | tf_op jit(solution)/shard_map/gather | solution.py:101
  92.0 1.9 %gather_fusion.15 = s32[256]{0:T(256)S(1)} fusion(s32[512]{0:T(512)S(1)} %copy-done, s32[1024]{0:T(1024)S(1)} %pad_clamp_fusion.10), kind=kCustom, calls=%fused_computation.15 | custom fusion | bytes 3072 | tf_op jit(solution)/shard_map/gather | solution.py:102
  93.9 1.9 %gather_fusion.9 = s32[256]{0:T(256)S(1)} fusion(s32[512]{0:T(512)S(1)} %copy-done.1, s32[1024]{0:T(1024)S(1)} %pad_clamp_fusion.10), kind=kCustom, calls=%fused_computation.9 | custom fusion | bytes 3072 | tf_op jit(solution)/shard_map/gather | solution.py:101
  95.9 1.9 %gather_fusion.30 = s32[256]{0:T(256)S(1)} fusion(s32[512]{0:T(512)S(1)} %copy-done, s32[1024]{0:T(1024)S(1)} %pad_clamp_fusion.3), kind=kCustom, calls=%fused_computation.30 | custom fusion | bytes 3072 | tf_op jit(solution)/shard_map/gather | solution.py:102
  97.9 1.9 %gather_fusion.24 = s32[256]{0:T(256)S(1)} fusion(s32[512]{0:T(512)S(1)} %copy-done.1, s32[1024]{0:T(1024)S(1)} %pad_clamp_fusion.3), kind=kCustom, calls=%fused_computation.24 | custom fusion | bytes 3072 | tf_op jit(solution)/shard_map/gather | solution.py:101
  99.8 1.9 %gather_fusion.31 = s32[256]{0:T(256)S(1)} fusion(s32[512]{0:T(512)S(1)} %copy-done, s32[1024]{0:T(1024)S(1)} %pad_clamp_fusion.2), kind=kCustom, calls=%fused_computation.31 | custom fusion | bytes 3072 | tf_op jit(solution)/shard_map/gather | solution.py:102
  101.8 1.9 %gather_fusion.25 = s32[256]{0:T(256)S(1)} fusion(s32[512]{0:T(512)S(1)} %copy-done.1, s32[1024]{0:T(1024)S(1)} %pad_clamp_fusion.2), kind=kCustom, calls=%fused_computation.25 | custom fusion | bytes 3072 | tf_op jit(solution)/shard_map/gather | solution.py:101
  104.1 19.3 %cosine_convert_fusion = (bf16[1152,256]{1,0:T(8,128)(2,1)S(1)}, bf16[1152,256]{1,0:T(8,128)(2,1)S(1)}, bf16[1152,256]{1,0:T(8,128)(2,1)S(1)}, bf16[1152,256]{1,...) fusion(s32[1152]{0:T(1024)S(1)} %add_select_fusion.8, ...), kind=kLoop, calls=%fused_computation.97 | loop fusion | flops 18874368 | bytes 4727296 | tf_op jit(solution)/shard_map/convert.2
  123.3 11.5 %subtract_convert_fusion = (bf16[256,640]{1,0:T(8,128)(2,1)S(1)}, bf16[256,640]{1,0:T(8,128)(2,1)S(1)}, bf16[256,640]{1,0:T(8,128)(2,1)S(1)}, bf16[256,640]{1,0:...) fusion(f32[256]{0:T(256)S(1)} %add_multiply_fusion, ...), kind=kLoop, calls=%fused_computation.137 | loop fusion | flops 15073280 | bytes 2636288 | tf_op jit(solution)/shard_map/convert
  141.2 6.1 %collective-permute-done = f32[1152,64]{0,1:T(8,128)S(1)} collective-permute-done((f32[1152,64]{0,1:T(8,128)S(1)}, f32[1152,64]{0,1:T(8,128)S(1)}, u32[]{:S(2)}, u32[]{:S(2)}) %collective-permute-start) | collective-permute-done | bytes 294944 | tf_op jit(solution)/shard_map/ppermute | solution.py:22
  149.4 4.1 %collective-permute-done.1 = f32[1152,64]{0,1:T(8,128)S(1)} collective-permute-done((f32[1152,64]{0,1:T(8,128)S(1)}, f32[1152,64]{0,1:T(8,128)S(1)}, u32[]{:S(2)}, u32[]{:S(2)}) %collective-permute-start.1) | collective-permute-done | bytes 294944 | tf_op jit(solution)/shard_map/ppermute | solution.py:23
  153.7 2.4 %collective-permute-start.2 = (f32[64,512]{0,1:T(8,128)S(1)}, f32[64,512]{0,1:T(8,128)S(1)}, u32[]{:S(2)}, u32[]{:S(2)}) collective-permute-start(f32[64,512]{0,1:T(8,128)S(1)} %pad_maximum_fusion.3), channel_id=1, source_target_pairs={{0,8},{8,16},{16,24},{1,9},{9,17},{17,25},{2,10},{10,18},{18,26},{... | collective-permute-start | bytes 393224 | tf_op jit(solution)/shard_map/ppermute | solution.py:22
  156.1 8.9 %collective-permute-done.2 = f32[64,512]{0,1:T(8,128)S(1)} collective-permute-done((f32[64,512]{0,1:T(8,128)S(1)}, f32[64,512]{0,1:T(8,128)S(1)}, u32[]{:S(2)}, u32[]{:S(2)}) %collective-permute-start.2) | collective-permute-done | bytes 131104 | tf_op jit(solution)/shard_map/ppermute | solution.py:22
  165.2 2.4 %collective-permute-start.3 = (f32[64,512]{0,1:T(8,128)S(1)}, f32[64,512]{0,1:T(8,128)S(1)}, u32[]{:S(2)}, u32[]{:S(2)}) collective-permute-start(f32[64,512]{0,1:T(8,128)S(1)} %get-tuple-element.20), channel_id=1, source_target_pairs={{8,0},{16,8},{24,16},{9,1},{17,9},{25,17},{10,2},{18,10},{26,18},{... | collective-permute-start | bytes 393224 | tf_op jit(solution)/shard_map/ppermute | solution.py:23
  169.2 6.5 %collective-permute-done.3 = f32[64,512]{0,1:T(8,128)S(1)} collective-permute-done((f32[64,512]{0,1:T(8,128)S(1)}, f32[64,512]{0,1:T(8,128)S(1)}, u32[]{:S(2)}, u32[]{:S(2)}) %collective-permute-start.3) | collective-permute-done | bytes 131104 | tf_op jit(solution)/shard_map/ppermute | solution.py:23
  (86 shorter events, 47.3 us)
Async XLA Ops:
  0.0 72.4 %copy-start = (s32[512]{0:T(512)S(1)}, s32[512]{0:T(512)}, u32[]{:S(2)}) copy-start(s32[512]{0:T(512)} %param.11) | copy-start | bytes 6148
  72.3 4.0 %copy-start.1 = (s32[512]{0:T(512)S(1)}, s32[512]{0:T(512)}, u32[]{:S(2)}) copy-start(s32[512]{0:T(512)} %param.10) | copy-start | bytes 6148
  139.3 8.0 %collective-permute-start = (f32[1152,64]{0,1:T(8,128)S(1)}, f32[1152,64]{0,1:T(8,128)S(1)}, u32[]{:S(2)}, u32[]{:S(2)}) collective-permute-start(f32[1152,64]{0,1:T(8,128)S(1)} %slice.321), channel_id=1, source_target_pairs={{0,1},{1,2},{2,3},{3,4},{4,5},{5,6},{6,7},{8,9},{9,10},{10,11},{11... | collective-permute-start | bytes 884744 | tf_op jit(solution)/shard_map/ppermute | solution.py:22
  147.4 6.1 %collective-permute-start.1 = (f32[1152,64]{0,1:T(8,128)S(1)}, f32[1152,64]{0,1:T(8,128)S(1)}, u32[]{:S(2)}, u32[]{:S(2)}) collective-permute-start(f32[1152,64]{0,1:T(8,128)S(1)} %get-tuple-element.18), channel_id=1, source_target_pairs={{1,0},{2,1},{3,2},{4,3},{5,4},{6,5},{7,6},{9,8},{10,9},{11,10},{12... | collective-permute-start | bytes 884744 | tf_op jit(solution)/shard_map/ppermute | solution.py:23
  153.7 11.3 %collective-permute-start.2 = (f32[64,512]{0,1:T(8,128)S(1)}, f32[64,512]{0,1:T(8,128)S(1)}, u32[]{:S(2)}, u32[]{:S(2)}) collective-permute-start(f32[64,512]{0,1:T(8,128)S(1)} %pad_maximum_fusion.3), channel_id=1, source_target_pairs={{0,8},{8,16},{16,24},{1,9},{9,17},{17,25},{2,10},{10,18},{18,26},{... | collective-permute-start | bytes 393224 | tf_op jit(solution)/shard_map/ppermute | solution.py:22
  165.2 10.6 %collective-permute-start.3 = (f32[64,512]{0,1:T(8,128)S(1)}, f32[64,512]{0,1:T(8,128)S(1)}, u32[]{:S(2)}, u32[]{:S(2)}) collective-permute-start(f32[64,512]{0,1:T(8,128)S(1)} %get-tuple-element.20), channel_id=1, source_target_pairs={{8,0},{16,8},{24,16},{9,1},{17,9},{25,17},{10,2},{18,10},{26,18},{... | collective-permute-start | bytes 393224 | tf_op jit(solution)/shard_map/ppermute | solution.py:23
  167.8 1.4 copy-start.2
  175.7 1.5 slice-start
where the time goes:
time: 180 us
  local copies, waits for them, and re-layouts  64.5 us (36%)
  blocking collectives  41.3 us (23%)
  other arithmetic  34.4 us (19%)
  waiting for transfers between devices  25.6 us (14%)
  starting transfers between devices  8.71 us (5%)
  matrix products  4.44 us (2%)
    psum x1, blocking collectives, shards(): gathered = lax.psum(slotted, ('frow', 'fcol'))  41.3 us
    another operation x2, other arithmetic  30.7 us
    gather x8, local copies, waits for them, and re-layouts, shards(): frequency_u = station_u_cells[tag_names[0]] - station_u_cells[tag_names[1]]  15.6 us
    gather x8, local copies, waits for them, and re-layouts, shards(): frequency_v = station_v_cells[tag_names[0]] - station_v_cells[tag_names[1]]  15.6 us
    ppermute x2, waiting for transfers between devices, extended_2(): before = lax.ppermute(last, axis, up)  15 us
    ppermute x2, waiting for transfers between devices, extended_2(): after = lax.ppermute(leading, axis, down)  10.6 us
    gather x4, local copies, waits for them, and re-layouts, block_weights(): g1r = g_tab[0][first]  6.89 us
    gather x4, local copies, waits for them, and re-layouts, block_weights(): g2r = g_tab[0][second]  6.89 us
  transfers between devices with their start and end apart: 4, of which 4 were waited for; matrix products, arithmetic and copies ran while one was open for 0% of the time, Pallas kernels for 0%

commit v1 on v0

v1 whole, which is shorter than its diff:
```python
import functools
import math

import jax
import jax.numpy as jnp
from jax import lax
from jax.experimental import pallas as pl
from jax.experimental.pallas import tpu as pltpu
from jax.sharding import PartitionSpec as P

R = 1024
C = 512
M = 64
NT = 16
NBLK = 4
LANES = 128
SUB = 8
OWN = 0
LEFT, RIGHT, UP, DOWN, UL, UR, DL, DR = range(1, 9)
F32 = jnp.float32
BF16 = jnp.bfloat16


def wrap(m, modulus):
    if modulus & (modulus - 1) == 0:
        return m & (modulus - 1)
    return jnp.remainder(m, modulus)


def turn(m, modulus):
    m = wrap(m, modulus)
    quarter = modulus // 4
    q = (m + modulus // 8) // quarter if quarter & (quarter - 1) else (
        (m + modulus // 8) >> (quarter.bit_length() - 1))
    x = (m - q * quarter).astype(F32) * (2.0 * math.pi / modulus)
    x2 = x * x
    s = x + x * x2 * (-1 / 6 + x2 * (1 / 120 + x2 * (-1 / 5040 + x2 * (1 / 362880))))
    c = 1.0 + x2 * (-0.5 + x2 * (1 / 24 + x2 * (-1 / 720 + x2 * (1 / 40320))))
    odd = (q & 1) == 1
    cos = jnp.where(odd, s, c)
    sin = jnp.where(odd, c, s)
    cos = jnp.where(((q + 1) & 2) != 0, -cos, cos)
    sin = jnp.where((q & 2) != 0, -sin, sin)
    return cos, sin


def times(a, b):
    return a[0] * b[0] - a[1] * b[1], a[0] * b[1] + a[1] * b[0]


def pack_kernel(g_ref, vis_ref, pair_ref, slot_ref, out_ref):
    depth = g_ref.shape[0]
    tail = jnp.concatenate(
        [vis_ref[...], pair_ref[...].astype(F32), slot_ref[...].astype(F32)], 0)
    for copy in range(out_ref.shape[0]):
        out_ref[copy, :depth, :] = g_ref[...]
        out_ref[copy, depth:depth + tail.shape[0], :] = tail


def image_kernel(n_frow, n_fcol, order_ref, mid_ref, left_ref, right_ref, block_ref,
                 u_ref, v_ref, out_ref,
                 s_ref, w_ref, uv_ref, dr_ref, ac_ref, as_ref, tc_ref, ts_ref,
                 uc_ref, us_ref, cc_ref, cs_ref, m1_ref, m2_ref, g1_ref, g2_ref):
    frow_at = lax.axis_index("frow")
    fcol_at = lax.axis_index("fcol")
    half_r, half_c = R // 2, C // 2
    mod_r, mod_c = 2 * R * n_frow, 2 * C * n_fcol
    k_tiles = s_ref.shape[1]
    per_block = k_tiles // NBLK
    shape = (SUB, LANES)

    for b in range(NBLK):
        owner = order_ref[b]
        for q in range(5):
            s_ref[q, b * per_block:(b + 1) * per_block, :] = block_ref[
                owner % n_fcol, owner // n_fcol, q * per_block:(q + 1) * per_block, :]
    a1 = s_ref[2].astype(jnp.int32)
    a2 = s_ref[3].astype(jnp.int32)
    slot = s_ref[4].astype(jnp.int32)

    def pick(row, lane):
        return jnp.take_along_axis(
            jnp.broadcast_to(row, shape), lane, axis=1, mode="promise_in_bounds")

    def cells(table):
        got = [jnp.zeros(shape, jnp.int32)] * 2
        for h in range(table.shape[0]):
            row = table[h:h + 1, :]
            got = [jnp.where((a >> 7) == h, pick(row, a & 127), g)
                   for a, g in zip((a1, a2), got)]
        return got[0] - got[1]

    u = cells(u_ref)
    v = cells(v_ref)
    uv_ref[0] = u
    uv_ref[1] = v

    i1 = a1 * NT + slot
    i2 = a2 * NT + slot
    h1, l1, h2, l2 = i1 >> 7, i1 & 127, i2 >> 7, i2 & 127
    above = jnp.maximum(frow_at - 1, 0)
    below = jnp.minimum(frow_at + 1, n_frow - 1)
    places = [None] * 9
    for row, names in ((frow_at, (LEFT, OWN, RIGHT)), (above, (UL, UP, UR)), (below, (DL, DOWN, DR))):
        for ref, name in zip((left_ref, mid_ref, right_ref), names):
            places[name] = (ref, row)
    steps = 512 * NT // LANES

    def gather(h, acc):
        m1, m2 = h1 == h, h2 == h
        new = []
        for f in range(9):
            ref, row = places[f]
            for comp in range(2):
                line = ref[row, pl.ds(2 * h + comp, 1), :]
                at = 4 * f + 2 * comp
                new.append(jnp.where(m1, pick(line, l1), acc[at]))
                new.append(jnp.where(m2, pick(line, l2), acc[at + 1]))
        return tuple(new)

    acc = lax.fori_loop(0, steps, gather, tuple([jnp.zeros(shape, F32)] * 36), unroll=2)

    centre = times(turn(u * (frow_at * (2 * R) + (R - 1)), mod_r),
                   turn(v * (fcol_at * (2 * C) + (C - 1)), mod_c))
    scale = 0.5 / math.sqrt(NBLK * per_block * LANES)
    value = times((s_ref[0] * scale, s_ref[1] * scale), centre)
    has_up = (frow_at > 0).astype(F32)
    has_down = (frow_at < n_frow - 1).astype(F32)
    for f in range(9):
        g1r, g2r, g1i, g2i = acc[4 * f:4 * f + 4]
        w = times(value, (g1r * g2r + g1i * g2i, g1i * g2r - g1r * g2i))
        keep = {UP: has_up, UL: has_up, UR: has_up,
                DOWN: has_down, DL: has_down, DR: has_down}.get(f)
        for comp in range(2):
            w_ref[2 * f + comp] = w[comp] if keep is None else w[comp] * keep

    iota = lax.broadcasted_iota(jnp.int32, shape, 0)

    def tapers(group, half):
        index = (iota + SUB * group).astype(F32)
        return ((half + M - 0.5 - index) * (1.0 / (2 * M)),
                (index - (half - M - 0.5)) * (1.0 / (2 * M)))

    zero = jnp.zeros((M, LANES), BF16)

    def tables(s, carry):
        lane = pl.ds(pl.multiple_of(s * LANES, LANES), LANES)

        def weight(f):
            return tuple(jnp.broadcast_to(w_ref[2 * f + comp, pl.ds(s, 1), :], shape)
                         for comp in range(2))

        def phases(which, modulus, half):
            freq = jnp.broadcast_to(uv_ref[which, pl.ds(s, 1), :], shape)
            fine = turn(freq * (2 * iota + 1), modulus)
            middle = turn(freq * (16 * iota), modulus)
            coarse = turn(freq * (128 * iota), modulus)
            for a in range(half // 64):
                top = tuple(jnp.broadcast_to(x[a:a + 1], shape) for x in coarse)
                both = times(middle, top)
                for comp in range(2):
                    dr_ref[which, comp, 8 * a:8 * a + 8, :] = both[comp]
            for g in range(half // SUB):
                step = tuple(jnp.broadcast_to(dr_ref[which, comp, g:g + 1, :], shape)
                             for comp in range(2))
                yield times(fine, step)

        pairs = {}

        def put(ref, first, group, x):
            key = (id(ref), first)
            if group % 2 == 0:
                pairs[key] = x
            else:
                start = first + SUB * (group - 1)
                ref[start:start + 16, lane] = jnp.concatenate([pairs.pop(key), x], 0).astype(BF16)

        edge = (half_r - M) // SUB
        rows_w = [weight(f) for f in (UP, DOWN, UL, UR, DL, DR)]
        signs = (-1, 1, -1, -1, 1, 1)
        for g, (cos, sin) in enumerate(phases(0, mod_r, half_r)):
            if g < edge:
                put(ac_ref, 0, g, cos)
                put(as_ref, 0, g, sin)
            else:
                mine, other = tapers(g, half_r)
                put(ac_ref, 0, g, cos * mine)
                put(as_ref, 0, g, sin * mine)
                cos, sin = cos * other, sin * other
                for n, ((wr, wi), sd) in enumerate(zip(rows_w, signs)):
                    put(uc_ref, n * M, g - edge, wr * cos - (sd * wi) * sin)
                    put(us_ref, n * M, g - edge, -(sd * wr) * sin - wi * cos)
        edge = (half_c - M) // SUB
        (wr, wi), (lr, li), (rr, ri) = weight(OWN), weight(LEFT), weight(RIGHT)
        for g, (cos, sin) in enumerate(phases(1, mod_c, half_c)):
            put(cc_ref, 0, g, cos)
            put(cs_ref, 0, g, sin)
            if g < edge:
                own = (cos, sin)
            else:
                mine, other = tapers(g, half_c)
                own = (cos * mine, sin * mine)
                cos, sin = cos * other, sin * other
                at = 2 * half_c + M
                put(tc_ref, at, g - edge, lr * cos + li * sin)
                put(ts_ref, at, g - edge, lr * sin - li * cos)
                put(tc_ref, at + 2 * M, g - edge, rr * cos - ri * sin)
                put(ts_ref, at + 2 * M, g - edge, -(rr * sin + ri * cos))
            put(tc_ref, 0, g, wr * own[0])
            put(tc_ref, half_c, g, -wi * own[1])
            put(ts_ref, 0, g, -wi * own[0])
            put(ts_ref, half_c, g, -wr * own[1])
        for ref in (tc_ref, ts_ref):
            ref[2 * half_c:2 * half_c + M, lane] = zero
            ref[2 * half_c + 2 * M:2 * half_c + 3 * M, lane] = zero
        return carry

    lax.fori_loop(0, k_tiles, tables, 0)

    def dot(a, b):
        return lax.dot_general(a[...], b[...], (((1,), (1,)), ((), ())), preferred_element_type=F32)

    m1_ref[...] = dot(ac_ref, tc_ref)
    m2_ref[...] = dot(as_ref, ts_ref)
    g1_ref[...] = dot(uc_ref, cc_ref)
    g2_ref[...] = dot(us_ref, cs_ref)

    lane_at = lax.broadcasted_iota(jnp.int32, shape, 1)
    back_lane = (LANES - 1) - lane_at
    back_row = (SUB - 1) - iota
    n_lane = half_c // LANES
    edge_c = half_c - M
    edge_r = half_r - M
    col_own, col_other = [], []
    for t in range(n_lane):
        index = (lane_at + t * LANES).astype(F32)
        col_own.append(jnp.minimum((half_c + M - 0.5 - index) * (1.0 / (2 * M)), 1.0))
        col_other.append(jnp.maximum((index - (half_c - M - 0.5)) * (1.0 / (2 * M)), 0.0))

    def flip(x, index, axis):
        return jnp.take_along_axis(x, index, axis=axis, mode="promise_in_bounds")

    def finish(g, edged):
        rows = pl.ds(pl.multiple_of(g * SUB, SUB), SUB)
        for t in range(n_lane):
            def part(ref, which):
                return ref[rows, which * half_c + t * LANES:which * half_c + (t + 1) * LANES]
            p, s_, r, q = part(m1_ref, 0), part(m1_ref, 1), part(m2_ref, 0), part(m2_ref, 1)
            even, odd = p + q, p - q
            plus, minus = r + s_, r - s_
            quad = {(1, 1): even + plus, (-1, -1): even - plus,
                    (1, -1): odd + minus, (-1, 1): odd - minus}
            if (t + 1) * LANES > edge_c:
                base = 2 * half_c
                off = t * LANES - (half_c - LANES)
                for se, start in ((-1, base), (1, base + LANES)):
                    lc = m1_ref[rows, start + off:start + off + LANES]
                    ls = m2_ref[rows, start + off:start + off + LANES]
                    quad[1, se] += lc + ls
                    quad[-1, se] += lc - ls
            if edged:
                def edge(n):
                    at = pl.ds(pl.multiple_of(n * M + g * SUB - edge_r, SUB), SUB)
                    x = g1_ref[at, t * LANES:(t + 1) * LANES]
                    y = g2_ref[at, t * LANES:(t + 1) * LANES]
                    return {1: x + y, -1: x - y}
                for n, sd in ((0, -1), (1, 1)):
                    e = edge(n)
                    for se in (-1, 1):
                        quad[sd, se] += e[se] * col_own[t]
                if (t + 1) * LANES > edge_c:
                    for n, (sd, se) in ((2, (-1, -1)), (3, (-1, 1)), (4, (1, -1)), (5, (1, 1))):
                        quad[sd, se] += edge(n)[se] * col_other[t]
            for (sd, se), x in quad.items():
                if sd < 0:
                    x = flip(x, back_row, 0)
                    at = pl.ds(pl.multiple_of(half_r - SUB - g * SUB, SUB), SUB)
                else:
                    at = pl.ds(pl.multiple_of(half_r + g * SUB, SUB), SUB)
                if se < 0:
                    x = flip(x, back_lane, 1)
                    start = half_c - (t + 1) * LANES
                else:
                    start = half_c + t * LANES
                out_ref[at, start:start + LANES] = x

    def inner(g, carry):
        finish(g, False)
        return carry

    def outer(g, carry):
        finish(g, True)
        return carry

    lax.fori_loop(0, edge_r // SUB, inner, 0, unroll=2)
    lax.fori_loop(edge_r // SUB, half_r // SUB, outer, 0)


def shards(vis, station_pairs, visibility_time_slot, station_u_cells, station_v_cells,
           facet_station_gains, holder_device_order):
    n_frow = lax.axis_size("frow")
    n_fcol = lax.axis_size("fcol")
    block = vis.shape[1]
    per_block = block // LANES
    k_tiles = NBLK * per_block
    k = k_tiles * LANES

    def lines(x):
        return x.reshape(-1, LANES)

    gains = facet_station_gains[0, 0]
    depth = gains.size // LANES
    g_lines = gains.reshape(2, -1, LANES).transpose(1, 0, 2).reshape(depth, LANES)
    tail = 16 * -(-5 * per_block // 16)
    packed = pl.pallas_call(
        pack_kernel,
        out_shape=jax.ShapeDtypeStruct((n_frow, depth + tail, LANES), F32),
        name="pack",
    )(g_lines, lines(vis), lines(station_pairs), lines(visibility_time_slot))
    mine = lax.all_to_all(packed, "frow", 0, 0)
    blocks = jnp.broadcast_to(mine[None, :, depth:], (n_fcol, n_frow, tail, LANES))
    blocks = lax.all_to_all(blocks, "fcol", 0, 0)
    up = [(i, i + 1) for i in range(n_fcol - 1)]
    left = lax.ppermute(mine, "fcol", up)
    right = lax.ppermute(mine, "fcol", [(j, i) for i, j in up])
    vmem = pl.BlockSpec(memory_space=pltpu.VMEM)
    half_r, half_c = R // 2, C // 2
    wide = 2 * half_c + 4 * M
    return pl.pallas_call(
        functools.partial(image_kernel, n_frow, n_fcol),
        out_shape=jax.ShapeDtypeStruct((R, C), F32),
        in_specs=[pl.BlockSpec(memory_space=pltpu.SMEM)] + [vmem] * 6,
        out_specs=vmem,
        scratch_shapes=[
            pltpu.VMEM((5, k_tiles, LANES), F32),
            pltpu.VMEM((18, k_tiles, LANES), F32),
            pltpu.VMEM((2, k_tiles, LANES), jnp.int32),
            pltpu.VMEM((2, 2, half_r // SUB, LANES), F32),
            pltpu.VMEM((half_r, k), BF16),
            pltpu.VMEM((half_r, k), BF16),
            pltpu.VMEM((wide, k), BF16),
            pltpu.VMEM((wide, k), BF16),
            pltpu.VMEM((6 * M, k), BF16),
            pltpu.VMEM((6 * M, k), BF16),
            pltpu.VMEM((half_c, k), BF16),
            pltpu.VMEM((half_c, k), BF16),
            pltpu.VMEM((half_r, wide), F32),
            pltpu.VMEM((half_r, wide), F32),
            pltpu.VMEM((6 * M, half_c), F32),
            pltpu.VMEM((6 * M, half_c), F32),
        ],
        compiler_params=pltpu.CompilerParams(vmem_limit_bytes=40 * 1024 * 1024),
        name="image",
    )(holder_device_order, mine, left, right, blocks,
      lines(station_u_cells), lines(station_v_cells))


def solution(mesh):
    return jax.shard_map(
        shards,
        mesh=mesh,
        in_specs=(
            P(None, ("frow", "fcol")),
            P(None, ("frow", "fcol")),
            P(("frow", "fcol")),
            P(),
            P(),
            P("frow", "fcol", None, None),
            P(),
        ),
        out_specs=P("frow", "fcol"),
        check_vma=False,
    )
```

time: 180 us -> 49.3 us (0.27)
  the two profiles are of different devices: /device:TPU:12 before, /device:TPU:1 now
where the time goes in v1:
time: 49.3 us; the launch traced here: 48.8 us
  Pallas kernels  16.6 us (34%)
  starting transfers between devices  12.4 us (25%)
  blocking collectives  9.59 us (19%)
  local copies, waits for them, and re-layouts  5.31 us (11%)
  waiting for transfers between devices  4.93 us (10%)
    pallas_call x1, Pallas kernels, shards(): pl.pallas_call(functools.partial(image_kernel, n_frow, n_fcol), out_shape...  15 us
    all_to_all x1, blocking collectives, shards(): mine = lax.all_to_all(packed, 'frow', 0, 0)  9.59 us
    all_to_all x1, starting transfers between devices, shards(): blocks = lax.all_to_all(blocks, 'fcol', 0, 0)  6.83 us
    ppermute x1, waiting for transfers between devices, shards(): right = lax.ppermute(mine, 'fcol', [(j, i) for i, j in up])  4.92 us
    ppermute x1, starting transfers between devices, shards(): left = lax.ppermute(mine, 'fcol', up)  3.64 us
    reshape x2, local copies, waits for them, and re-layouts, lines(): return x.reshape(-1, LANES)  2.56 us
    unnamed x6, local copies, waits for them, and re-layouts  2.02 us
    ppermute x1, starting transfers between devices, shards(): right = lax.ppermute(mine, 'fcol', [(j, i) for i, j in up])  1.91 us
  transfers between devices with their start and end apart: 3, of which 1 were waited for; matrix products, arithmetic and copies ran while one was open for 0% of the time, Pallas kernels for 0%

profile of v1, /device:TPU:1, one launch (start us, length us, event | category | flops | bytes accessed | tf_op | source)
XLA Modules:
  0.0 48.8 jit_solution(6955849448809230780)
XLA Ops:
  0.0 1.3 %reshape.20.vis_ref = f32[4,128]{1,0:T(4,128)} reshape(f32[2,256]{1,0:T(2,128)} %param.7) | data formatting | bytes 4096 | tf_op jit(solution)/shard_map/reshape | solution.py:309
  1.3 1.3 %reshape.21.pair_ref = s32[4,128]{1,0:T(4,128)} reshape(s32[2,256]{1,0:T(2,128)} %param.8) | data formatting | bytes 4096 | tf_op jit(solution)/shard_map/reshape | solution.py:309
  2.6 1.6 %pack.1 = f32[4,144,128]{2,1,0:T(8,128)} custom-call(f32[128,128]{1,0:T(8,128)} %bitcast.10, f32[4,128]{1,0:T(4,128)} %reshape.20.vis_ref, s32[4,128]{1,0:T(4,128)} %reshape.21.pair_ref, s32[2,128]{1,0:T(2,128)} %bitcast.11), custom_call_target="tpu_custom_call" | custom-call | tf_op jit(solution)/shard_map/pack/pallas_call | solution.py:315
  4.1 9.6 %all_to_all.10.mid_ref = f32[4,144,128]{2,1,0:T(8,128)S(1)} all-to-all(f32[4,144,128]{2,1,0:T(8,128)} %pack.1), channel_id=1, replica_groups=mesh['frow'=4,'fcol'=8] {'frow'}, dimensions={0} | all-to-all | bytes 589824 | tf_op jit(solution)/shard_map/all_to_all | solution.py:320
  13.7 0.7 %broadcast_in_dim.2 = f32[8,4,16,128]{3,2,1,0:T(8,128)} broadcast(f32[4,16,128]{2,1,0:T(8,128)S(1)} %slice.4), dimensions={1,2,3} | broadcast | bytes 294912 | tf_op jit(solution)/shard_map/broadcast_in_dim | solution.py:321
  14.5 6.8 %all-to-all-start.1 = ((f32[8,4,16,128]{3,2,1,0:T(8,128)}), f32[8,4,16,128]{3,2,1,0:T(8,128)S(1)}, u32[]{:S(2)}, u32[]{:S(2)}) async-start(f32[8,4,16,128]{3,2,1,0:T(8,128)} %broadcast_in_dim.2), calls=%async_computation.1 | async-start | bytes 524288 | tf_op jit(solution)/shard_map/all_to_all | solution.py:322
  21.3 1.9 %collective-permute-start.1 = (f32[4,144,128]{2,1,0:T(8,128)S(1)}, f32[4,144,128]{2,1,0:T(8,128)S(1)}, u32[]{:S(2)}, u32[]{:S(2)}) collective-permute-start(f32[4,144,128]{2,1,0:T(8,128)S(1)} %all_to_all.10.mid_ref), channel_id=1, source_target_pairs={{1,0},{2,1},{3,2},{4,3},{5,4},{6,5},{7,6},{9,8},{10,9},{11,10},{12... | collective-permute-start | bytes 884744 | tf_op jit(solution)/shard_map/ppermute | solution.py:325
  23.2 3.6 %collective-permute-start = (f32[4,144,128]{2,1,0:T(8,128)S(1)}, f32[4,144,128]{2,1,0:T(8,128)S(1)}, u32[]{:S(2)}, u32[]{:S(2)}) collective-permute-start(f32[4,144,128]{2,1,0:T(8,128)S(1)} %all_to_all.10.mid_ref), channel_id=1, source_target_pairs={{0,1},{1,2},{2,3},{3,4},{4,5},{5,6},{6,7},{8,9},{9,10},{10,11},{11... | collective-permute-start | bytes 884744 | tf_op jit(solution)/shard_map/ppermute | solution.py:324
  26.9 4.9 %collective-permute-done.1.right_ref = f32[4,144,128]{2,1,0:T(8,128)S(1)} collective-permute-done((f32[4,144,128]{2,1,0:T(8,128)S(1)}, f32[4,144,128]{2,1,0:T(8,128)S(1)}, u32[]{:S(2)}, u32[]{:S(2)}) %collective-permute-start.1) | collective-permute-done | bytes 294944 | tf_op jit(solution)/shard_map/ppermute | solution.py:325
  31.8 0.0 collective-permute-done.left_ref
  31.8 0.0 all-to-all-done.1.block_ref
  31.8 0.0 copy-start
  31.8 0.7 %copy-done = s32[512]{0:T(512)S(1)} copy-done((s32[512]{0:T(512)S(1)}, s32[512]{0:T(512)}, u32[]{:S(2)}) %copy-start) | copy-done | bytes 2072
  32.5 0.0 copy-start.1
  32.5 0.7 %copy-done.1 = s32[512]{0:T(512)S(1)} copy-done((s32[512]{0:T(512)S(1)}, s32[512]{0:T(512)}, u32[]{:S(2)}) %copy-start.1) | copy-done | bytes 2072
  33.2 0.0 copy-start.2
  33.2 0.7 %copy-done.2 = s32[32]{0:T(128)S(1)} copy-done((s32[32]{0:T(128)S(1)}, s32[32]{0:T(128)}, u32[]{:S(2)}) %copy-start.2) | copy-done | bytes 152
  33.8 15.0 %image.1 = f32[1024,512]{1,0:T(8,128)} custom-call(s32[32]{0:T(128)S(1)} %copy-done.2, f32[4,144,128]{2,1,0:T(8,128)S(1)} %all_to_all.10.mid_ref, f32[4,144,128]{2,1,0:T(8,128)S(1)} %collective-permute-done.left_ref, f32[4,144,128]{2,1,0:T(8,128)S(1)} %collective-permute-done.1.right_ref, f32[8,4,16,128]{3,2,1,0:T(8,128)S(1)} %all-to-all-done.1.block_ref, ...), custom_call_target="tpu_custom_call" | custom-call | tf_op jit(solution)/shard_map/image/pallas_call | solution.py:329
  (1 shorter events, 0.0 us)
Async XLA Ops:
  14.5 17.3 %all-to-all-start.1 = ((f32[8,4,16,128]{3,2,1,0:T(8,128)}), f32[8,4,16,128]{3,2,1,0:T(8,128)S(1)}, u32[]{:S(2)}, u32[]{:S(2)}) async-start(f32[8,4,16,128]{3,2,1,0:T(8,128)} %broadcast_in_dim.2), calls=%async_computation.1 | async-start | bytes 524288 | tf_op jit(solution)/shard_map/all_to_all | solution.py:322
  21.3 10.5 %collective-permute-start.1 = (f32[4,144,128]{2,1,0:T(8,128)S(1)}, f32[4,144,128]{2,1,0:T(8,128)S(1)}, u32[]{:S(2)}, u32[]{:S(2)}) collective-permute-start(f32[4,144,128]{2,1,0:T(8,128)S(1)} %all_to_all.10.mid_ref), channel_id=1, source_target_pairs={{1,0},{2,1},{3,2},{4,3},{5,4},{6,5},{7,6},{9,8},{10,9},{11,10},{12... | collective-permute-start | bytes 884744 | tf_op jit(solution)/shard_map/ppermute | solution.py:325
  23.2 8.6 %collective-permute-start = (f32[4,144,128]{2,1,0:T(8,128)S(1)}, f32[4,144,128]{2,1,0:T(8,128)S(1)}, u32[]{:S(2)}, u32[]{:S(2)}) collective-permute-start(f32[4,144,128]{2,1,0:T(8,128)S(1)} %all_to_all.10.mid_ref), channel_id=1, source_target_pairs={{0,1},{1,2},{2,3},{3,4},{4,5},{5,6},{6,7},{8,9},{9,10},{10,11},{11... | collective-permute-start | bytes 884744 | tf_op jit(solution)/shard_map/ppermute | solution.py:324
  31.8 0.7 %copy-start = (s32[512]{0:T(512)S(1)}, s32[512]{0:T(512)}, u32[]{:S(2)}) copy-start(s32[512]{0:T(512)} %param.10) | copy-start | bytes 6148
  32.5 0.7 %copy-start.1 = (s32[512]{0:T(512)S(1)}, s32[512]{0:T(512)}, u32[]{:S(2)}) copy-start(s32[512]{0:T(512)} %param.11) | copy-start | bytes 6148
  33.2 0.7 %copy-start.2 = (s32[32]{0:T(128)S(1)}, s32[32]{0:T(128)}, u32[]{:S(2)}) copy-start(s32[32]{0:T(128)} %order_ref.1) | copy-start | bytes 388
